TPU v7x, 32 devices: a whole 2x2x4 slice. The times are simulated.
32 devices in a mesh: groups: 2 (over x), expert: 16 (over z, y, core).
Axes of the slice: x: 2, y: 2, z: 4, core: 2. Of those that a mesh axis runs over, the one named last changes fastest.
Arguments:
- act: bfloat16 [4096, 7168], P(('groups', 'expert')), parts along dimension 0, may hold values from -6 to 6
- act_scale: bfloat16 [4096], P(('groups', 'expert')), parts along dimension 0, may hold values from 0.29882812 to 3
- route_ids: int32 [4096, 2], P(('groups', 'expert')), parts along dimension 0, may hold values from 0 to 7, all different within a row; in each aligned block of 128 rows (0 to 127, 128 to 255, ...) at most 64 rows name the same one
- route_weights: float32 [4096, 2], P(('groups', 'expert')), parts along dimension 0, may hold values from 0.2 to 1
- w_gate: bfloat16 [16, 7168, 512], P('expert'), may hold values from -127 to 127
- w_up: bfloat16 [16, 7168, 512], P('expert'), may hold values from -127 to 127
- w_down: bfloat16 [16, 512, 7168], P('expert'), may hold values from -127 to 127
- gate_scale: float32 [16, 512], P('expert'), may hold values from 8e-05 to 0.00032
- up_scale: float32 [16, 512], P('expert'), may hold values from 8e-05 to 0.00032
- down_scale: float32 [8, 7168], replicated, may hold values from 0.0004 to 0.0016
Outputs:
- mixed: bfloat16 [4096, 7168], P(('groups', 'expert')), parts along dimension 0
There are 2 independent parts, one for each index of `groups`. A program takes and returns all parts, laid end to end along the dimension named above; an argument that names none is the same for every part. Nothing has to cross between parts.
Inputs may be any that keep to these rules, and one draw needn't show every extreme that they name: `route_ids`: each row names 2 different experts; among the rows of one device no expert is named by more than 64 rows, a bound that some block reaches.
All inputs are finite; a program needn't handle non-finite values.
Results may differ from a plain program's by a relative error of at most 0.0066.
Values may be sent and summed in bfloat16 or wider, within the bound.
A program may use at most 128 MiB of HBM per device.

v0:
```python
import jax
import jax.numpy as jnp
from jax import lax
from jax.sharding import PartitionSpec as P

PIECES = 2
TOP = 2


def from_partner(value, axis, stride):
    return lax.ppermute(value, axis, [(i, i ^ 1 << stride) for i in range(lax.axis_size(axis))])


def expert_rows(rows, scales, wg, wu, wd, gscale, uscale, down_row):
    shape = rows.shape
    flat = rows.reshape(-1, shape[-1])
    factor = scales.reshape(-1, 1).astype(jnp.float32)
    gate = jnp.dot(flat, wg, preferred_element_type=jnp.float32) * factor * gscale[None, :]
    upper = jnp.dot(flat, wu, preferred_element_type=jnp.float32) * factor * uscale[None, :]
    hidden = (jax.nn.silu(gate) * upper).astype(jnp.bfloat16)
    partial_value = jnp.dot(hidden, wd, preferred_element_type=jnp.float32) * down_row[None, :]
    return partial_value.astype(jnp.bfloat16).reshape(shape)


def body(
    act, act_scale, route_ids, route_weights, w_gate, w_up, w_down, gate_scale, up_scale, down_scale
):
    tok_rows = act.shape[0]
    width = act.shape[1]
    devices = lax.axis_size("expert")
    experts = down_scale.shape[0]
    capacity = 2 * tok_rows * TOP // experts
    owner = lax.axis_index("expert") // PIECES
    down_row = lax.dynamic_index_in_dim(down_scale, owner, 0, keepdims=False)
    wg = w_gate[0]
    wu = w_up[0]
    wd = w_down[0]
    gscale = gate_scale[0]
    uscale = up_scale[0]
    flat_ids = route_ids.reshape(-1)
    routes = flat_ids.shape[0]
    onehot = (flat_ids[:, None] == jnp.arange(experts, dtype=jnp.int32)[None, :]).astype(jnp.int32)
    before = jnp.cumsum(onehot, axis=0) - onehot
    rank = jnp.sum(before * onehot, axis=1)
    target = flat_ids * capacity + rank
    hit = (jnp.arange(experts * capacity, dtype=jnp.int32)[:, None] == target[None, :]).astype(
        jnp.int32
    )
    filled = jnp.sum(hit, axis=1) > 0
    route_of_slot = jnp.sum(hit * jnp.arange(routes, dtype=jnp.int32)[None, :], axis=1)
    token_of_slot = route_of_slot // TOP
    send_rows = jnp.where(filled[:, None], act[token_of_slot], jnp.zeros((), jnp.bfloat16))
    send_scales = jnp.where(filled, act_scale[token_of_slot], jnp.zeros((), jnp.bfloat16))
    half = capacity // 2
    split_rows = send_rows.reshape(devices, half, width)
    split_scales = send_scales.reshape(devices, half)
    own_rows = lax.all_to_all(split_rows, "expert", split_axis=0, concat_axis=0, tiled=True)
    own_scales = lax.all_to_all(split_scales, "expert", split_axis=0, concat_axis=0, tiled=True)
    other_rows, other_scales = from_partner((own_rows, own_scales), "expert", 0)
    items = own_rows.shape[1]
    both_rows = jnp.concatenate([own_rows, other_rows], axis=1)
    both_scales = jnp.concatenate([own_scales, other_scales], axis=1)
    part = expert_rows(both_rows, both_scales, wg, wu, wd, gscale, uscale, down_row)
    mine = part[:, :items]
    theirs = part[:, items:]
    arrived = from_partner(theirs, "expert", 0)
    total = (mine.astype(jnp.float32) + arrived.astype(jnp.float32)).astype(jnp.bfloat16)
    back = lax.all_to_all(total, "expert", split_axis=0, concat_axis=0, tiled=True)
    expert_out = back.reshape(experts * capacity, width)
    picked = jnp.take(expert_out, target, axis=0).reshape(tok_rows, TOP, width)
    mixed = jnp.zeros((tok_rows, width), jnp.float32)
    for position in range(TOP):
        mixed = mixed + route_weights[:, position][:, None] * picked[:, position].astype(
            jnp.float32
        )
    return mixed.astype(jnp.bfloat16)


def solution(mesh):
    return jax.shard_map(
        body,
        mesh=mesh,
        in_specs=(
            P(("groups", "expert"), None),
            P(("groups", "expert")),
            P(("groups", "expert"), None),
            P(("groups", "expert"), None),
            P("expert", None, None),
            P("expert", None, None),
            P("expert", None, None),
            P("expert", None),
            P("expert", None),
            P(),
        ),
        out_specs=P(("groups", "expert"), None),
        check_vma=False,
    )
```

profile of v0, /device:TPU:13, one launch (start us, length us, event | category | flops | bytes accessed | tf_op | source)
XLA Modules:
  0.0 457.0 jit_solution(15874217335716720982)
XLA Ops:
  0.0 0.9 copy.29
  0.9 0.1 eq.39
  1.1 0.1 reshape.193
  1.2 0.6 reduce-window.6
  1.8 0.2 slice_reduce_fusion
  2.1 0.1 fusion.10
  2.2 0.2 convert_reduce_fusion
  2.4 3.5 gather_fusion.1
  5.9 0.1 gt.20
  6.0 0.0 copy-done
  6.0 7.1 %gather_fusion = bf16[512,7168]{1,0:T(8,128)(2,1)} fusion(bf16[128,7168]{1,0:T(8,128)(2,1)S(1)} %copy-done, s32[1024]{0:T(1024)S(1)} %pad_clamp_fusion.1), kind=kCustom, calls=%fused_computation | custom fusion | bytes 14682112 | tf_op jit(solution)/shard_map/gather | solution.py:52
  13.1 3.6 broadcast_select_fusion
  16.7 166.1 %all_to_all.19 = bf16[16,32,7168]{2,1,0:T(8,128)(2,1)} all-to-all(bf16[16,32,7168]{2,1,0:T(8,128)(2,1)S(1)} %broadcast_select_fusion), channel_id=1, replica_groups=mesh['groups'=2,'expert'=16] {'expert'}, dimensions={0} | all-to-all | bytes 14680064 | tf_op jit(solution)/shard_map/all_to_all | solution.py:57
  182.8 0.2 collective-permute-start
  183.0 0.7 select_n.84
  183.7 5.7 %all-to-all-start.1 = ((bf16[16,1,32]{2,1,0:T(2,128)(2,1)}), bf16[16,1,32]{2,1,0:T(2,128)(2,1)S(1)}, u32[]{:S(2)}, u32[]{:S(2)}) async-start(bf16[16,1,32]{2,1,0:T(2,128)(2,1)} %select_n.84), calls=%async_computation.1 | async-start | bytes 16384 | tf_op jit(solution)/shard_map/all_to_all | solution.py:58
  189.4 5.1 %all-to-all-done.1 = bf16[16,1,32]{2,1,0:T(2,128)(2,1)S(1)} async-done(((bf16[16,1,32]{2,1,0:T(2,128)(2,1)}), bf16[16,1,32]{2,1,0:T(2,128)(2,1)S(1)}, u32[]{:S(2)}, u32[]{:S(2)}) %all-to-all-start.1) | async-done | bytes 1056 | tf_op jit(solution)/shard_map/all_to_all | solution.py:58
  194.6 0.2 collective-permute-start.1
  194.8 1.0 constant_dynamic-slice_fusion
  195.8 0.0 collective-permute-done.1
  195.8 0.1 maximum_convert_fusion
  195.8 0.1 reshape.198
  195.9 0.0 collective-permute-done
  195.9 7.9 %pad_maximum_fusion = bf16[16,64,7168]{2,1,0:T(8,128)(2,1)S(1)} fusion(bf16[16,32,7168]{2,1,0:T(8,128)(2,1)} %collective-permute-done, bf16[16,32,7168]{2,1,0:T(8,128)(2,1)} %all_to_all.19), kind=kLoop, calls=%fused_computation.4 | loop fusion | flops 29360128 | bytes 29360128 | tf_op jit(solution)/shard_map/concatenate | solution.py:61
  203.8 0.0 slice-start.1
  203.8 0.0 copy-start.4
  203.8 0.0 copy-start.5
  203.8 11.2 %fusion.3 = f32[1024,512]{1,0:T(8,128)} fusion(bf16[1024,7168]{1,0:T(8,128)(2,1)S(1)} %bitcast.51, bf16[1,7168,512]{2,1,0:T(8,128)(2,1)} %param.14), kind=kOutput, calls=%fused_computation.9 | convolution fusion | flops 7516192768 | bytes 24117248 | tf_op jit(solution)/shard_map/dot_general | solution.py:18
  215.0 0.0 slice-done
  215.0 0.0 copy-done.4
  215.0 9.5 %multiply_convert_fusion.1 = bf16[1024,512]{1,0:T(8,128)(2,1)S(1)} fusion(f32[1024,512]{1,0:T(8,128)} %fusion.3, bf16[1024,7168]{1,0:T(8,128)(2,1)S(1)} %bitcast.52, bf16[1,7168,512]{2,1,0:T(8,128)(2,1)S(1)} %bitcast.63, f32[512]{0:T(512)S(1)} %bitcast.64, f32[512]{0:T(512)S(1)} %bitcast.65, f32[1024]{0:T(1024)S(1)} %reshape.198), kind=kOutput, calls=%fused_computation.17 | convolution fusion | flops 7521435648 | bytes 25174016 | tf_op jit(solution)/shard_map/dot_general | solution.py:19
  224.5 14.4 %multiply_convert_fusion = bf16[1024,7168]{1,0:T(8,128)(2,1)} fusion(bf16[1024,512]{1,0:T(8,128)(2,1)S(1)} %multiply_convert_fusion.1, f32[7168]{0:T(1024)S(1)} %bitcast.55, bf16[1,512,7168]{2,1,0:T(8,128)(2,1)} %param.16), kind=kOutput, calls=%fused_computation.3 | convolution fusion | flops 7530872832 | bytes 23097344 | tf_op jit(solution)/shard_map/dot_general | solution.py:21
  238.9 3.7 slice.40
  242.6 0.4 collective-permute-start.2
  243.0 11.5 %collective-permute-done.2 = bf16[16,32,7168]{2,1,0:T(8,128)(2,1)} collective-permute-done((bf16[16,32,7168]{2,1,0:T(8,128)(2,1)S(1)}, bf16[16,32,7168]{2,1,0:T(8,128)(2,1)}, u32[]{:S(2)}, u32[]{:S(2)}) %collective-permute-start.2) | collective-permute-done | bytes 7340064 | tf_op jit(solution)/shard_map/ppermute | solution.py:11
  254.5 10.9 %add_convert_fusion = bf16[16,32,7168]{2,1,0:T(8,128)(2,1)} fusion(bf16[16,32,7168]{2,1,0:T(8,128)(2,1)} %collective-permute-done.2, bf16[16,64,7168]{2,1,0:T(8,128)(2,1)} %bitcast.54), kind=kLoop, calls=%fused_computation.5 | loop fusion | flops 14680064 | bytes 22020096 | tf_op jit(solution)/shard_map/convert_element_type | solution.py:67
  265.4 5.9 %all-to-all-start.2 = ((bf16[16,32,7168]{2,1,0:T(8,128)(2,1)}), bf16[16,32,7168]{2,1,0:T(8,128)(2,1)}, u32[]{:S(2)}, u32[]{:S(2)}) async-start(bf16[16,32,7168]{2,1,0:T(8,128)(2,1)} %add_convert_fusion), calls=%async_computation.2 | async-start | bytes 14680064 | tf_op jit(solution)/shard_map/all_to_all | solution.py:68
  271.2 0.1 reduce_sum.34
  271.4 0.1 copy.33
  271.5 0.1 mul.132
  271.6 0.1 copy.31
  271.7 0.0 copy-done.3
  271.8 159.3 %all-to-all-done.2 = bf16[16,32,7168]{2,1,0:T(8,128)(2,1)} async-done(((bf16[16,32,7168]{2,1,0:T(8,128)(2,1)}), bf16[16,32,7168]{2,1,0:T(8,128)(2,1)}, u32[]{:S(2)}, u32[]{:S(2)}) %all-to-all-start.2) | async-done | bytes 7340064 | tf_op jit(solution)/shard_map/all_to_all | solution.py:68
  431.1 12.1 %gather_fusion.2 = bf16[256,7168]{1,0:T(8,128)(2,1)} fusion(bf16[512,7168]{1,0:T(8,128)(2,1)} %bitcast.14, s32[1024]{0:T(1024)S(1)} %pad_clamp_fusion), kind=kCustom, calls=%fused_computation.2 | custom fusion | bytes 7341056 | tf_op jit(solution)/shard_map/jit(_take)/gather | solution.py:70
  443.3 8.3 %gather.18 = bf16[128,2,7168]{2,1,0:T(2,128)(2,1)} reshape(bf16[256,7168]{1,0:T(8,128)(2,1)} %gather_fusion.2) | data formatting | bytes 7340032 | tf_op jit(solution)/shard_map/jit(_take)/gather | solution.py:70
  451.5 3.5 copy_select_fusion
  455.0 2.0 fusion.6
  457.0 0.0 copy-done.1
  (22 shorter events, 0.1 us)
Async XLA Ops:
  0.0 6.0 %copy-start = (bf16[128,7168]{1,0:T(8,128)(2,1)S(1)}, bf16[128,7168]{1,0:T(8,128)(2,1)}, u32[]{:S(2)}) copy-start(bf16[128,7168]{1,0:T(8,128)(2,1)} %param.10) | copy-start | bytes 5505028
  182.8 13.1 %collective-permute-start = (bf16[16,32,7168]{2,1,0:T(8,128)(2,1)}, bf16[16,32,7168]{2,1,0:T(8,128)(2,1)}, u32[]{:S(2)}, u32[]{:S(2)}) collective-permute-start(bf16[16,32,7168]{2,1,0:T(8,128)(2,1)} %all_to_all.19), channel_id=1, source_target_pairs={{0,1},{1,0},{2,3},{3,2},{4,5},{5,4},{6,7},{7,6},{8,9},{9,8},{10,11... | collective-permute-start | bytes 22020104 | tf_op jit(solution)/shard_map/ppermute | solution.py:11
  183.7 10.9 %all-to-all-start.1 = ((bf16[16,1,32]{2,1,0:T(2,128)(2,1)}), bf16[16,1,32]{2,1,0:T(2,128)(2,1)S(1)}, u32[]{:S(2)}, u32[]{:S(2)}) async-start(bf16[16,1,32]{2,1,0:T(2,128)(2,1)} %select_n.84), calls=%async_computation.1 | async-start | bytes 16384 | tf_op jit(solution)/shard_map/all_to_all | solution.py:58
  194.6 1.2 collective-permute-start.1
  195.9 19.1 %slice-start = ((s8[7340032]{0:T(1024)(128)(4,1)}), s8[4194304]{0:T(1024)(128)(4,1)S(1)}, s32[]{:S(2)}) async-start(s8[7340032]{0:T(1024)(128)(4,1)} %bitcast.62), calls=%async_computation.3 | async-start | bytes 8388608
  203.8 11.2 %slice-start.1 = ((s8[7340032]{0:T(1024)(128)(4,1)}), s8[3145728]{0:T(1024)(128)(4,1)S(1)}, s32[]{:S(2)}) async-start(s8[7340032]{0:T(1024)(128)(4,1)} %bitcast.62), calls=%async_computation.4 | async-start | bytes 6291456
  203.8 11.2 %copy-start.4 = (f32[1,512]{1,0:T(1,128)S(1)}, f32[1,512]{1,0:T(1,128)}, u32[]{:S(2)}) copy-start(f32[1,512]{1,0:T(1,128)} %param.18) | copy-start | bytes 6148
  203.8 11.2 %copy-start.5 = (f32[1,512]{1,0:T(1,128)S(1)}, f32[1,512]{1,0:T(1,128)}, u32[]{:S(2)}) copy-start(f32[1,512]{1,0:T(1,128)} %param.17) | copy-start | bytes 6148
  242.6 11.9 %collective-permute-start.2 = (bf16[16,32,7168]{2,1,0:T(8,128)(2,1)S(1)}, bf16[16,32,7168]{2,1,0:T(8,128)(2,1)}, u32[]{:S(2)}, u32[]{:S(2)}) collective-permute-start(bf16[16,32,7168]{2,1,0:T(8,128)(2,1)S(1)} %slice.40), channel_id=1, source_target_pairs={{0,1},{1,0},{2,3},{3,2},{4,5},{5,4},{6,7},{7,6},{8,9},{9,8},{10,11... | collective-permute-start | bytes 22020104 | tf_op jit(solution)/shard_map/ppermute | solution.py:11
  265.4 6.0 %copy-start.2 = (s32[128,2]{0,1:T(2,128)S(1)}, s32[128,2]{0,1:T(2,128)}, u32[]{:S(2)}) copy-start(s32[128,2]{0,1:T(2,128)} %param.12) | copy-start | bytes 3076
  265.4 6.4 %copy-start.3 = (f32[128,2]{0,1:T(2,128)S(1)}, f32[128,2]{0,1:T(2,128)}, u32[]{:S(2)}) copy-start(f32[128,2]{0,1:T(2,128)} %param.13) | copy-start | bytes 3076
  265.4 165.8 %all-to-all-start.2 = ((bf16[16,32,7168]{2,1,0:T(8,128)(2,1)}), bf16[16,32,7168]{2,1,0:T(8,128)(2,1)}, u32[]{:S(2)}, u32[]{:S(2)}) async-start(bf16[16,32,7168]{2,1,0:T(8,128)(2,1)} %add_convert_fusion), calls=%async_computation.2 | async-start | bytes 14680064 | tf_op jit(solution)/shard_map/all_to_all | solution.py:68
  443.3 13.7 %copy-start.1 = (bf16[128,7168]{1,0:T(8,128)(2,1)S(1)}, bf16[128,7168]{1,0:T(8,128)(2,1)}, u32[]{:S(2)}) copy-start(bf16[128,7168]{1,0:T(8,128)(2,1)} %param.10) | copy-start | bytes 5505028
where the time goes:
time: 458 us; the launch traced here: 457 us
  waiting for transfers between devices  176 us (38%)
  blocking collectives  166 us (36%)
  local copies, waits for them, and re-layouts  38.3 us (8%)
  matrix products  35 us (8%)
  other arithmetic  29 us (6%)
  starting transfers between devices  12.4 us (3%)
    all_to_all x1, blocking collectives, body(): lax.all_to_all(split_rows, 'expert', split_axis=0, concat_axis=0, tiled=T...  166 us
    all_to_all x1, waiting for transfers between devices, body(): lax.all_to_all(total, 'expert', split_axis=0, concat_axis=0, tiled=True)  159 us
    gather x2, local copies, waits for them, and re-layouts, body(): picked = jnp.take(expert_out, target, axis=0).reshape(tok_rows, TOP, width)  20.4 us
    dot_general x1, matrix products, expert_rows(): jnp.dot(hidden, wd, preferred_element_type=jnp.float32) * down_row[None, :]  14.4 us
    ppermute x3, waiting for transfers between devices, from_partner(): lax.ppermute(value, axis, [(i, i ^ 1 << stride) for i in range(lax.axis_s...  11.5 us
    dot_general x1, matrix products, expert_rows(): jnp.dot(flat, wg, preferred_element_type=jnp.float32) * factor  11.2 us
    convert_element_type x1, other arithmetic, body(): (mine.astype(jnp.float32) + arrived.astype(jnp.float32)).astype(jnp.bfloa...  10.9 us
    dot_general x1, matrix products, expert_rows(): jnp.dot(flat, wu, preferred_element_type=jnp.float32) * factor  9.47 us
  transfers between devices with their start and end apart: 5, of which 3 were waited for; matrix products, arithmetic and copies ran while one was open for 1% of the time, Pallas kernels for 0%

commit v1 on v0

v1 whole, which is shorter than its diff:
```python
import jax
import jax.numpy as jnp
from jax import lax
from jax.sharding import PartitionSpec as P

PIECES = 2


def body(
    act, act_scale, route_ids, route_weights, w_gate, w_up, w_down, gate_scale, up_scale, down_scale
):
    owner = lax.axis_index("expert") // PIECES
    down_row = lax.dynamic_index_in_dim(down_scale, owner, 0, keepdims=False)
    rows = lax.all_gather(act, "expert", axis=0, tiled=True)
    scales = lax.all_gather(act_scale, "expert", axis=0, tiled=True)
    ids = lax.all_gather(route_ids, "expert", axis=0, tiled=True)
    weights = lax.all_gather(route_weights, "expert", axis=0, tiled=True)
    hit = ids == owner
    weight = jnp.sum(jnp.where(hit, weights, 0.0), axis=1)
    factor = scales[:, None].astype(jnp.float32)
    gate = jnp.dot(rows, w_gate[0], preferred_element_type=jnp.float32) * factor * gate_scale[0][None, :]
    upper = jnp.dot(rows, w_up[0], preferred_element_type=jnp.float32) * factor * up_scale[0][None, :]
    hidden = (jax.nn.silu(gate) * upper).astype(jnp.bfloat16)
    part = jnp.dot(hidden, w_down[0], preferred_element_type=jnp.float32) * down_row[None, :]
    part = (part * weight[:, None]).astype(jnp.bfloat16)
    return lax.psum_scatter(part, "expert", scatter_dimension=0, tiled=True)


def solution(mesh):
    return jax.shard_map(
        body,
        mesh=mesh,
        in_specs=(
            P(("groups", "expert"), None),
            P(("groups", "expert")),
            P(("groups", "expert"), None),
            P(("groups", "expert"), None),
            P("expert", None, None),
            P("expert", None, None),
            P("expert", None, None),
            P("expert", None),
            P("expert", None),
            P(),
        ),
        out_specs=P(("groups", "expert"), None),
        check_vma=False,
    )
```

time: 458 us -> 511 us (1.12)
  waiting for transfers between devices: 176 us -> 373 us
  blocking collectives: 166 us -> 54.9 us
  local copies, waits for them, and re-layouts: 38.3 us -> 0.05 us
  matrix products: 35 us -> 66.1 us
  other arithmetic: 29 us -> 0.04 us
  between operations: 0.21 us -> 13.5 us
  starting transfers between devices: 12.4 us -> 0.04 us
    reduce_scatter x0 -> x1, waiting for transfers between devices: none -> 276 us  [body(): return lax.psum_scatter(part, 'expert', scatter_dimension=0, tiled=True)]
    all_to_all x1 -> x0, blocking collectives: 166 us -> none  [body(): lax.all_to_all(split_rows, 'expert', split_axis=0, concat_axis=0, tiled=T...]
    all_to_all x2 -> x0, waiting for transfers between devices: 164 us -> none  [the longest x1 159 us: body(): lax.all_to_all(total, 'expert', split_axis=0, concat_axis=0, tiled=True)]
    all_gather x0 -> x1, waiting for transfers between devices: none -> 96.4 us  [body(): rows = lax.all_gather(act, 'expert', axis=0, tiled=True)]
    all_gather x0 -> x3, blocking collectives: none -> 54.9 us  [the longest x1 21.6 us: body(): weights = lax.all_gather(route_weights, 'expert', axis=0, tiled=True)]
    dot_general x3, matrix products: 35 us -> 66.1 us  [the longest x1 22.6 us: body(): jnp.dot(rows, w_gate[0], preferred_element_type=jnp.float32) * factor]
    gather x4 -> x0, local copies, waits for them, and re-layouts: 30.9 us -> none  [the longest x2 20.4 us: body(): picked = jnp.take(expert_out, target, axis=0).reshape(tok_rows, TOP, width)]
    convert_element_type x4 -> x1, other arithmetic: 13 us -> 0.01 us  [body(): factor = scales[:, None].astype(jnp.float32)]
  transfers between devices with their start and end apart: 5 -> 2, of which waited for: 3 -> 2; matrix products, arithmetic and copies ran while one was open for 1% -> 0% of each run, Pallas kernels for 0% -> 0%
where the time goes in v1:
time: 511 us; the launch traced here: 508 us
  waiting for transfers between devices  373 us (73%)
  matrix products  66.1 us (13%)
  blocking collectives  54.9 us (11%)
  between operations  13.5 us (3%)
    reduce_scatter x1, waiting for transfers between devices, body(): return lax.psum_scatter(part, 'expert', scatter_dimension=0, tiled=True)  276 us
    all_gather x1, waiting for transfers between devices, body(): rows = lax.all_gather(act, 'expert', axis=0, tiled=True)  96.4 us
    dot_general x1, matrix products, body(): jnp.dot(rows, w_gate[0], preferred_element_type=jnp.float32) * factor  22.6 us
    dot_general x1, matrix products, body(): jnp.dot(hidden, w_down[0], preferred_element_type=jnp.float32)  22.5 us
    all_gather x1, blocking collectives, body(): weights = lax.all_gather(route_weights, 'expert', axis=0, tiled=True)  21.6 us
    dot_general x1, matrix products, body(): jnp.dot(rows, w_up[0], preferred_element_type=jnp.float32) * factor  21 us
    all_gather x1, blocking collectives, body(): ids = lax.all_gather(route_ids, 'expert', axis=0, tiled=True)  17.7 us
    all_gather x1, blocking collectives, body(): scales = lax.all_gather(act_scale, 'expert', axis=0, tiled=True)  15.6 us
  transfers between devices with their start and end apart: 2, of which 2 were waited for; matrix products, arithmetic and copies ran while one was open for 0% of the time, Pallas kernels for 0%

profile of v1, /device:TPU:13, one launch (start us, length us, event | category | flops | bytes accessed | tf_op | source)
XLA Modules:
  0.0 507.5 jit_solution(2097301642504051374)
XLA Ops:
  6.5 0.0 copy-start
  6.5 0.0 all-gather.3.cloned.1.call-start
  6.5 0.7 all-gather.3.cloned.1.call-update
  7.3 0.0 reduce-scatter.2.cloned.1.call-start
  7.3 15.6 %all-gather = bf16[16,1,128]{2,1,0:T(2,128)(2,1)S(1)} all-gather(bf16[1,1,128]{2,1,0:T(2,128)(2,1)} %bitcast.21), channel_id=1, replica_groups=mesh['groups'=2,'expert'=16] {'expert'}, dimensions={0}, use_global_device_ids=true | all-gather | bytes 4352 | tf_op jit(solution)/shard_map/all_gather | solution.py:15
  23.0 21.6 %all_gather.15 = f32[2048,2]{0,1:T(2,128)S(1)} all-gather(f32[128,2]{0,1:T(2,128)} %param.13), channel_id=1, replica_groups=mesh['groups'=2,'expert'=16] {'expert'}, dimensions={0}, use_global_device_ids=true | all-gather | bytes 17408 | tf_op jit(solution)/shard_map/all_gather | solution.py:17
  44.6 17.7 %all_gather.14 = s32[2048,2]{0,1:T(2,128)S(1)} all-gather(s32[128,2]{0,1:T(2,128)} %param.12), channel_id=1, replica_groups=mesh['groups'=2,'expert'=16] {'expert'}, dimensions={0}, use_global_device_ids=true | all-gather | bytes 17408 | tf_op jit(solution)/shard_map/all_gather | solution.py:16
  62.3 0.0 copy-done
  62.3 0.0 copy-start.2
  62.4 0.0 copy-start.3
  62.4 96.4 %all-gather.3.cloned.1.call-done = bf16[2048,7168]{1,0:T(8,128)(2,1)} async-done(((bf16[128,7168]{1,0:T(8,128)(2,1)}), bf16[2048,7168]{1,0:T(8,128)(2,1)}) %all-gather.3.cloned.1.call-update) | async-done | bytes 29360144 | tf_op jit(solution)/shard_map/all_gather | solution.py:14
  158.8 21.0 %fusion.1 = f32[2048,512]{1,0:T(8,128)S(1)} fusion(bf16[2048,7168]{1,0:T(8,128)(2,1)} %all-gather.3.cloned.1.call-done, bf16[1,7168,512]{2,1,0:T(8,128)(2,1)} %param.15), kind=kOutput, calls=%fused_computation.2 | convolution fusion | flops 15032385536 | bytes 40894464 | tf_op jit(solution)/shard_map/dot_general | solution.py:22
  179.7 0.0 copy-done.2
  179.7 0.0 copy-done.3
  179.8 22.6 %multiply_convert_fusion.1 = bf16[2048,512]{1,0:T(8,128)(2,1)S(1)} fusion(f32[2048,512]{1,0:T(8,128)S(1)} %fusion.1, bf16[2048,7168]{1,0:T(8,128)(2,1)} %all-gather.3.cloned.1.call-done, bf16[1,7168,512]{2,1,0:T(8,128)(2,1)} %param.14, f32[512]{0:T(512)S(1)} %bitcast.22, f32[512]{0:T(512)S(1)} %bitcast.23, f32[2048]{0:T(1024)S(1)} %bitcast.20), kind=kOutput, calls=%fused_computation.6 | convolution fusion | flops 15042871296 | bytes 43003904 | tf_op jit(solution)/shard_map/dot_general | solution.py:21
  202.4 22.5 %multiply_convert_fusion = bf16[2048,7168]{1,0:T(8,128)(2,1)} fusion(bf16[2048,512]{1,0:T(8,128)(2,1)S(1)} %multiply_convert_fusion.1, f32[2048]{0:T(1024)S(1)} %fusion.7, f32[7168]{0:T(1024)S(1)} %bitcast.19, bf16[1,512,7168]{2,1,0:T(8,128)(2,1)} %param.16), kind=kOutput, calls=%fused_computation | convolution fusion | flops 15076425728 | bytes 38834176 | tf_op jit(solution)/shard_map/dot_general | solution.py:24
  224.9 0.0 reduce-scatter.2.cloned.1.call-update
  224.9 0.0 copy-start.1
  224.9 275.8 %reduce-scatter.2.cloned.1.call-done = bf16[128,7168]{1,0:T(8,128)(2,1)} async-done(((bf16[2048,7168]{1,0:T(8,128)(2,1)}), bf16[128,7168]{1,0:T(8,128)(2,1)}) %reduce-scatter.2.cloned.1.call-update) | async-done | bytes 1835024 | tf_op jit(solution)/shard_map/reduce_scatter | solution.py:26
  500.7 0.0 copy-done.1
  (3 shorter events, 0.1 us)
Async XLA Ops:
  6.5 55.8 %copy-start = (f32[8,7168]{1,0:T(8,128)S(1)}, f32[8,7168]{1,0:T(8,128)}, u32[]{:S(2)}) copy-start(f32[8,7168]{1,0:T(8,128)} %param.19) | copy-start | bytes 688132
  6.5 152.2 %all-gather.3.cloned.1.call-start = ((), (), s32[]{:S(2)}) async-start(), calls=%async_computation.1 | async-start | bytes 31195136 | tf_op jit(solution)/shard_map/all_gather | solution.py:14
  7.3 493.4 %reduce-scatter.2.cloned.1.call-start = ((), (), s32[]{:S(2)}) async-start(), calls=%async_computation.2 | async-start | bytes 31195136 | tf_op jit(solution)/shard_map/reduce_scatter | solution.py:26
  62.3 117.4 %copy-start.2 = (f32[1,512]{1,0:T(1,128)S(1)}, f32[1,512]{1,0:T(1,128)}, u32[]{:S(2)}) copy-start(f32[1,512]{1,0:T(1,128)} %param.18) | copy-start | bytes 6148
  62.4 117.4 %copy-start.3 = (f32[1,512]{1,0:T(1,128)S(1)}, f32[1,512]{1,0:T(1,128)}, u32[]{:S(2)}) copy-start(f32[1,512]{1,0:T(1,128)} %param.17) | copy-start | bytes 6148
  224.9 275.8 %copy-start.1 = (f32[8,7168]{1,0:T(8,128)S(1)}, f32[8,7168]{1,0:T(8,128)}, u32[]{:S(2)}) copy-start(f32[8,7168]{1,0:T(8,128)} %param.19) | copy-start | bytes 688132
Sparse Core Ops, SparseCore 0:
  9.0 149.7 all-gather.2
  225.0 275.6 reduce-scatter.1

commit v2 on v1

v2 whole, which is shorter than its diff:
```python
import functools
import math

import jax
import jax.numpy as jnp
from jax import lax
from jax.experimental import pallas as pl
from jax.experimental.pallas import tpu as pltpu
from jax.sharding import PartitionSpec as P

PIECES = 2
X_SLOTS = 4
ACC_SLOTS = 3


def kernel(
    n, snake, experts, x_hbm, wg_hbm, wu_hbm, wd_hbm, gs_ref, us_ref, down_ref, out_ref,
    xb, acc_in, acc_out, sp_in, sp_out, wg, wu, wd, hid,
    load_sem, x_send, x_recv, a_send, a_recv, sx_sem, sp_sem,
):
    rows, width = out_ref.shape
    half = rows // 2
    hidden = hid.shape[1]
    me = lax.axis_index("expert")
    core = me % 2
    chip = me // 2
    sib = chip * 2 + (1 - core)
    if snake:
        odd = chip % 2
        pos = (1 - odd) * (chip // 2) + odd * (n - 1 - chip // 2)
    else:
        pos = chip

    def device_at(p):
        p = p % n
        if snake:
            high = p // (n // 2)
            p = (1 - high) * (2 * p) + high * (2 * (n - 1 - p) + 1)
        return p * 2 + core

    ahead = device_at(pos + 1)
    behind = device_at(pos + n - 1)

    def remote(src, dst, send, recv, target):
        return pltpu.make_async_remote_copy(
            src_ref=src, dst_ref=dst, send_sem=send, recv_sem=recv,
            device_id={"expert": target}, device_id_type=pl.DeviceIdType.MESH,
        )

    def ring_x(s):
        a, b = s % X_SLOTS, (s + 1) % X_SLOTS
        return [
            remote(xb.at[a, pl.ds(d * half, half)], xb.at[b, pl.ds(d * half, half)],
                   x_send.at[d, a], x_recv.at[d, b], to)
            for d, to in enumerate((ahead, behind))
        ]

    def ring_acc(s):
        a, b = s % 2, (s + 1) % ACC_SLOTS
        return [
            remote(acc_out.at[a, pl.ds(d * half, half)], acc_in.at[b, pl.ds(d * half, half)],
                   a_send.at[d, a], a_recv.at[d, b], to)
            for d, to in enumerate((ahead, behind))
        ]

    def sib_x(s):
        a = s % X_SLOTS
        return remote(xb.at[a, pl.ds(0, rows)], xb.at[a, pl.ds(rows, rows)],
                      sx_sem.at[0, a], sx_sem.at[1, a], sib)

    def sib_part(s):
        a = s % 2
        return remote(sp_out.at[a], sp_in.at[a], sp_sem.at[0, a], sp_sem.at[1, a], sib)

    first = pltpu.make_async_copy(x_hbm, xb.at[0, pl.ds(0, rows)], load_sem.at[0])
    first.start()
    loads = [
        pltpu.make_async_copy(src, dst, load_sem.at[1 + i])
        for i, (src, dst) in enumerate(((wg_hbm, wg), (wu_hbm, wu), (wd_hbm, wd)))
    ]
    for load in loads:
        load.start()
    barrier = pltpu.get_barrier_semaphore()
    for other in (ahead, behind, sib):
        pl.semaphore_signal(barrier, inc=1, device_id={"expert": other},
                            device_id_type=pl.DeviceIdType.MESH)
    pl.semaphore_wait(barrier, 3)
    first.wait()

    tile = math.gcd(width, 512)
    htile = math.gcd(hidden, 256)

    def step(s, carry):
        slot = s % X_SLOTS
        out_slot = s % 2

        @pl.when(s >= 1)
        def _():
            for copy in ring_x(s - 1):
                copy.wait_recv()

        @pl.when(s >= 2)
        def _():
            for copy in ring_x(s - 2):
                copy.wait_send()

        @pl.when(s < n - 1)
        def _():
            for copy in ring_x(s):
                copy.start()

        to_sib = sib_x(s)
        to_sib.start()
        to_sib.wait()

        @pl.when(s == 0)
        def _():
            for load in loads:
                load.wait()

        @pl.when(s >= 3)
        def _():
            for copy in ring_acc(s - 2):
                copy.wait_send()

        meta = xb[slot, :, width:].astype(jnp.float32)
        lane = lax.broadcasted_iota(jnp.int32, meta.shape, 1)
        mine = (lane == chip) | (lane == experts + chip)
        weight = jnp.sum(jnp.where(mine, meta, 0.0), axis=1, keepdims=True)
        factor = jnp.sum(jnp.where(lane == 2 * experts, meta, 0.0), axis=1, keepdims=True)

        @pl.loop(0, hidden // htile)
        def _(j):
            cols = pl.ds(pl.multiple_of(j * htile, htile), htile)
            rows_x = xb[slot, :, :width]
            gate = jnp.dot(rows_x, wg[:, cols], preferred_element_type=jnp.float32)
            gate = gate * factor * gs_ref[:, cols]
            upper = jnp.dot(rows_x, wu[:, cols], preferred_element_type=jnp.float32)
            upper = upper * factor * us_ref[:, cols]
            hid[:, cols] = (gate / (1.0 + jnp.exp(-gate)) * upper).astype(jnp.bfloat16)

        @pl.loop(0, width // tile)
        def _(t):
            cols = pl.ds(pl.multiple_of(t * tile, tile), tile)
            part = jnp.dot(hid[...], wd[:, cols], preferred_element_type=jnp.float32)
            part = (part * down_ref[:, cols] * weight).astype(jnp.bfloat16)
            acc_out[out_slot, :, cols] = part[:rows]
            sp_out[out_slot, :, cols] = part[rows:]

        exchange = sib_part(s)
        exchange.start()
        exchange.wait()

        def both(cols):
            return acc_out[out_slot, :, cols].astype(jnp.float32) + sp_in[
                out_slot, :, cols
            ].astype(jnp.float32)

        @pl.when(s == 0)
        def _():
            @pl.loop(0, width // tile)
            def _(t):
                cols = pl.ds(pl.multiple_of(t * tile, tile), tile)
                out_ref[:, cols] = both(cols).astype(jnp.bfloat16)

        @pl.when(s == 1)
        def _():
            @pl.loop(0, width // tile)
            def _(t):
                cols = pl.ds(pl.multiple_of(t * tile, tile), tile)
                acc_out[out_slot, :, cols] = both(cols).astype(jnp.bfloat16)

        @pl.when(s >= 2)
        def _():
            for copy in ring_acc(s - 1):
                copy.wait_recv()
            in_slot = s % ACC_SLOTS

            @pl.loop(0, width // tile)
            def _(t):
                cols = pl.ds(pl.multiple_of(t * tile, tile), tile)
                total = both(cols) + acc_in[in_slot, :, cols].astype(jnp.float32)
                acc_out[out_slot, :, cols] = total.astype(jnp.bfloat16)

        @pl.when(s >= 1)
        def _():
            for copy in ring_acc(s):
                copy.start()

        return carry

    lax.fori_loop(0, n, step, 0)
    for copy in ring_acc(n - 1):
        copy.wait_recv()

    @pl.loop(0, width // tile)
    def _(t):
        cols = pl.ds(pl.multiple_of(t * tile, tile), tile)
        total = out_ref[:, cols].astype(jnp.float32) + acc_in[n % ACC_SLOTS, :, cols].astype(
            jnp.float32
        )
        out_ref[:, cols] = total.astype(jnp.bfloat16)

    for copy in ring_x(n - 2) + ring_acc(n - 2) + ring_acc(n - 1):
        copy.wait_send()


def body(
    snake, act, act_scale, route_ids, route_weights, w_gate, w_up, w_down, gate_scale, up_scale,
    down_scale
):
    rows, width = act.shape
    experts = down_scale.shape[0]
    hidden = w_gate.shape[2]
    n = lax.axis_size("expert") // PIECES
    owner = lax.axis_index("expert") // PIECES
    down_row = lax.dynamic_slice_in_dim(down_scale, owner, 1, 0)
    hit = route_ids[:, :, None] == jnp.arange(experts, dtype=jnp.int32)[None, None, :]
    dense = jnp.sum(jnp.where(hit, route_weights[:, :, None], 0.0), axis=1)
    high = lax.reduce_precision(dense, 8, 7)
    low = dense - high
    used = 2 * experts + 1
    extra = -(-used // 128) * 128
    meta = jnp.concatenate(
        [high.astype(jnp.bfloat16), low.astype(jnp.bfloat16), act_scale[:, None],
         jnp.zeros((rows, extra - used), jnp.bfloat16)], axis=1)
    x = jnp.concatenate([act, meta], axis=1)
    bf16 = jnp.bfloat16
    anywhere = pl.BlockSpec(memory_space=pl.ANY)
    vmem = pl.BlockSpec(memory_space=pltpu.VMEM)
    dma = pltpu.SemaphoreType.DMA
    return pl.pallas_call(
        functools.partial(kernel, n, snake, experts),
        out_shape=jax.ShapeDtypeStruct((rows, width), bf16),
        in_specs=[anywhere] * 4 + [vmem] * 3,
        out_specs=vmem,
        scratch_shapes=[
            pltpu.VMEM((X_SLOTS, 2 * rows, width + extra), bf16),
            pltpu.VMEM((ACC_SLOTS, rows, width), bf16),
            pltpu.VMEM((2, rows, width), bf16),
            pltpu.VMEM((2, rows, width), bf16),
            pltpu.VMEM((2, rows, width), bf16),
            pltpu.VMEM((width, hidden), bf16),
            pltpu.VMEM((width, hidden), bf16),
            pltpu.VMEM((hidden, width), bf16),
            pltpu.VMEM((2 * rows, hidden), bf16),
            dma((4,)), dma((2, X_SLOTS)), dma((2, X_SLOTS)),
            dma((2, 2)), dma((2, ACC_SLOTS)), dma((2, X_SLOTS)), dma((2, 2)),
        ],
        compiler_params=pltpu.CompilerParams(
            collective_id=0, has_side_effects=True, vmem_limit_bytes=62 * 1024 * 1024
        ),
    )(x, w_gate[0], w_up[0], w_down[0], gate_scale, up_scale, down_row)


def winds_back(mesh):
    chips = [getattr(d, "coords", None) for d in mesh.devices[0][::PIECES]]
    if any(c is None for c in chips):
        return False
    return sum(len({c[i] for c in chips}) > 1 for i in range(len(chips[0]))) == 2


def solution(mesh):
    return jax.shard_map(
        functools.partial(body, winds_back(mesh)),
        mesh=mesh,
        in_specs=(
            P(("groups", "expert"), None),
            P(("groups", "expert")),
            P(("groups", "expert"), None),
            P(("groups", "expert"), None),
            P("expert", None, None),
            P("expert", None, None),
            P("expert", None, None),
            P("expert", None),
            P("expert", None),
            P(),
        ),
        out_specs=P(("groups", "expert"), None),
        check_vma=False,
    )
```

time: 511 us -> 299 us (0.59)
  waiting for transfers between devices: 373 us -> 0 us
  Pallas kernels: 0 us -> 285 us
  matrix products: 66.1 us -> 0 us
  blocking collectives: 54.9 us -> 0 us
  between operations: 13.5 us -> 0.03 us
  local copies, waits for them, and re-layouts: 0.05 us -> 8.62 us
    pallas_call x0 -> x1, Pallas kernels: none -> 285 us  [body(): pl.pallas_call(functools.partial(kernel, n, snake, experts), out_shape=ja...]
    reduce_scatter x1 -> x0, waiting for transfers between devices: 276 us -> none  [body(): return lax.psum_scatter(part, 'expert', scatter_dimension=0, tiled=True)]
    all_gather x1 -> x0, waiting for transfers between devices: 96.4 us -> none  [body(): rows = lax.all_gather(act, 'expert', axis=0, tiled=True)]
    dot_general x3 -> x0, matrix products: 66.1 us -> none  [the longest x1 22.6 us: body(): jnp.dot(rows, w_gate[0], preferred_element_type=jnp.float32) * factor]
    all_gather x3 -> x0, blocking collectives: 54.9 us -> none  [the longest x1 21.6 us: body(): weights = lax.all_gather(route_weights, 'expert', axis=0, tiled=True)]
  transfers between devices with their start and end apart: 2 -> 0, of which waited for: 2 -> 0; matrix products, arithmetic and copies ran while one was open for 0% -> 0% of each run, Pallas kernels for 0% -> 0%
where the time goes in v2:
time: 299 us; the launch traced here: 294 us
  Pallas kernels  285 us (95%)
  local copies, waits for them, and re-layouts  8.62 us (3%)
    pallas_call x1, Pallas kernels, body(): pl.pallas_call(functools.partial(kernel, n, snake, experts), out_shape=ja...  285 us

profile of v2, /device:TPU:13, one launch (start us, length us, event | category | flops | bytes accessed | tf_op | source)
XLA Modules:
  0.0 294.3 jit_solution(1610097510944622904)
XLA Ops:
  0.0 0.0 copy-start
  0.0 0.7 select_reduce_fusion
  0.8 0.2 copy-done
  1.0 0.6 constant_dynamic-slice_fusion.down_ref
  1.6 0.1 copy.19
  1.7 0.8 copy.20
  2.5 0.1 copy.18
  2.6 0.1 copy.17
  2.7 3.8 %concatenate.3.x_hbm = bf16[128,7296]{1,0:T(8,128)(2,1)} concatenate(bf16[128,7168]{1,0:T(8,128)(2,1)} %param.10, bf16[128,8]{1,0:T(8,128)(2,1)S(1)} %copy.19, bf16[128,8]{1,0:T(8,128)(2,1)S(1)} %subtract_convert_fusion, bf16[128,1]{1,0:T(8,128)(2,1)S(1)} %copy.20, bf16[128,111]{1,0:T(8,128)(2,1)S(1)} %broadcast_in_dim.24), dimensions={1} | concatenate | bytes 3735552 | tf_op jit(solution)/shard_map/concatenate | solution.py:227
  6.6 284.9 %shard_map.100 = bf16[128,7168]{1,0:T(8,128)(2,1)} custom-call(bf16[128,7296]{1,0:T(8,128)(2,1)} %concatenate.3.x_hbm, bf16[7168,512]{1,0:T(8,128)(2,1)} %bitcast.4, bf16[7168,512]{1,0:T(8,128)(2,1)} %bitcast.5, bf16[512,7168]{1,0:T(8,128)(2,1)} %bitcast.6, f32[1,512]{1,0:T(1,128)} %gs_ref.1, f32[1,512]{1,0:T(1,128)} %us_ref.1, ...), custom_call_target="tpu_custom_call" | custom-call | tf_op jit(solution)/shard_map/pallas_call | solution.py:232
  291.5 2.8 copy.22
  (3 shorter events, 0.0 us)
Async XLA Ops:
  0.0 1.0 copy-start

commit v3 on v2

--- a/solution.py
+++ b/solution.py
@@ -11,10 +11,11 @@
 PIECES = 2
 X_SLOTS = 4
 ACC_SLOTS = 3
+BANDS = 2
 
 
 def kernel(
-    n, snake, experts, x_hbm, wg_hbm, wu_hbm, wd_hbm, gs_ref, us_ref, down_ref, out_ref,
+    n, snake, experts, x_hbm, meta_hbm, wg_hbm, wu_hbm, wd_hbm, gs_ref, us_ref, down_ref, out_ref,
     xb, acc_in, acc_out, sp_in, sp_out, wg, wu, wd, hid,
     load_sem, x_send, x_recv, a_send, a_recv, sx_sem, sp_sem,
 ):
@@ -55,11 +56,15 @@
             for d, to in enumerate((ahead, behind))
         ]
 
-    def ring_acc(s):
+    band = width // BANDS
+
+    def ring_acc(s, k):
         a, b = s % 2, (s + 1) % ACC_SLOTS
+        cols = pl.ds(k * band, band)
         return [
-            remote(acc_out.at[a, pl.ds(d * half, half)], acc_in.at[b, pl.ds(d * half, half)],
-                   a_send.at[d, a], a_recv.at[d, b], to)
+            remote(acc_out.at[a, pl.ds(d * half, half), cols],
+                   acc_in.at[b, pl.ds(d * half, half), cols],
+                   a_send.at[d, k, a], a_recv.at[d, k, b], to)
             for d, to in enumerate((ahead, behind))
         ]
 
@@ -72,10 +77,16 @@
         a = s % 2
         return remote(sp_out.at[a], sp_in.at[a], sp_sem.at[0, a], sp_sem.at[1, a], sib)
 
-    first = pltpu.make_async_copy(x_hbm, xb.at[0, pl.ds(0, rows)], load_sem.at[0])
-    first.start()
+    first = [
+        pltpu.make_async_copy(x_hbm, xb.at[0, pl.ds(0, rows), pl.ds(0, width)], load_sem.at[3]),
+        pltpu.make_async_copy(
+            meta_hbm, xb.at[0, pl.ds(0, rows), pl.ds(width, meta_hbm.shape[1])], load_sem.at[4]
+        ),
+    ]
+    for load in first:
+        load.start()
     loads = [
-        pltpu.make_async_copy(src, dst, load_sem.at[1 + i])
+        pltpu.make_async_copy(src, dst, load_sem.at[i])
         for i, (src, dst) in enumerate(((wg_hbm, wg), (wu_hbm, wu), (wd_hbm, wd)))
     ]
     for load in loads:
@@ -85,33 +96,20 @@
         pl.semaphore_signal(barrier, inc=1, device_id={"expert": other},
                             device_id_type=pl.DeviceIdType.MESH)
     pl.semaphore_wait(barrier, 3)
-    first.wait()
-
-    tile = math.gcd(width, 512)
+    for load in first:
+        load.wait()
+    for copy in ring_x(0):
+        copy.start()
+    sib_x(0).start()
+
+    tile = math.gcd(band, 512)
     htile = math.gcd(hidden, 256)
 
     def step(s, carry):
         slot = s % X_SLOTS
         out_slot = s % 2
 
-        @pl.when(s >= 1)
-        def _():
-            for copy in ring_x(s - 1):
-                copy.wait_recv()
-
-        @pl.when(s >= 2)
-        def _():
-            for copy in ring_x(s - 2):
-                copy.wait_send()
-
-        @pl.when(s < n - 1)
-        def _():
-            for copy in ring_x(s):
-                copy.start()
-
-        to_sib = sib_x(s)
-        to_sib.start()
-        to_sib.wait()
+        sib_x(s).wait()
 
         @pl.when(s == 0)
         def _():
@@ -120,8 +118,9 @@
 
         @pl.when(s >= 3)
         def _():
-            for copy in ring_acc(s - 2):
-                copy.wait_send()
+            for k in range(BANDS):
+                for copy in ring_acc(s - 2, k):
+                    copy.wait_send()
 
         meta = xb[slot, :, width:].astype(jnp.float32)
         lane = lax.broadcasted_iota(jnp.int32, meta.shape, 1)
@@ -139,6 +138,23 @@
             upper = upper * factor * us_ref[:, cols]
             hid[:, cols] = (gate / (1.0 + jnp.exp(-gate)) * upper).astype(jnp.bfloat16)
 
+        @pl.when(s < n - 1)
+        def _():
+            for copy in ring_x(s):
+                copy.wait_recv()
+
+            @pl.when(s >= 1)
+            def _():
+                for copy in ring_x(s - 1):
+                    copy.wait_send()
+
+            @pl.when(s < n - 2)
+            def _():
+                for copy in ring_x(s + 1):
+                    copy.start()
+
+            sib_x(s + 1).start()
+
         @pl.loop(0, width // tile)
         def _(t):
             cols = pl.ds(pl.multiple_of(t * tile, tile), tile)
@@ -163,46 +179,51 @@
                 cols = pl.ds(pl.multiple_of(t * tile, tile), tile)
                 out_ref[:, cols] = both(cols).astype(jnp.bfloat16)
 
-        @pl.when(s == 1)
-        def _():
-            @pl.loop(0, width // tile)
-            def _(t):
-                cols = pl.ds(pl.multiple_of(t * tile, tile), tile)
-                acc_out[out_slot, :, cols] = both(cols).astype(jnp.bfloat16)
-
-        @pl.when(s >= 2)
-        def _():
-            for copy in ring_acc(s - 1):
-                copy.wait_recv()
-            in_slot = s % ACC_SLOTS
-
-            @pl.loop(0, width // tile)
-            def _(t):
-                cols = pl.ds(pl.multiple_of(t * tile, tile), tile)
-                total = both(cols) + acc_in[in_slot, :, cols].astype(jnp.float32)
-                acc_out[out_slot, :, cols] = total.astype(jnp.bfloat16)
-
-        @pl.when(s >= 1)
-        def _():
-            for copy in ring_acc(s):
-                copy.start()
+        for k in range(BANDS):
+            @pl.when(s == 1)
+            def _():
+                @pl.loop(0, band // tile)
+                def _(t):
+                    cols = pl.ds(pl.multiple_of(k * band + t * tile, tile), tile)
+                    acc_out[out_slot, :, cols] = both(cols).astype(jnp.bfloat16)
+
+            @pl.when(s >= 2)
+            def _():
+                for copy in ring_acc(s - 1, k):
+                    copy.wait_recv()
+                in_slot = s % ACC_SLOTS
+
+                @pl.loop(0, band // tile)
+                def _(t):
+                    cols = pl.ds(pl.multiple_of(k * band + t * tile, tile), tile)
+                    total = both(cols) + acc_in[in_slot, :, cols].astype(jnp.float32)
+                    acc_out[out_slot, :, cols] = total.astype(jnp.bfloat16)
+
+            @pl.when(s >= 1)
+            def _():
+                for copy in ring_acc(s, k):
+                    copy.start()
 
         return carry
 
     lax.fori_loop(0, n, step, 0)
-    for copy in ring_acc(n - 1):
-        copy.wait_recv()
-
-    @pl.loop(0, width // tile)
-    def _(t):
-        cols = pl.ds(pl.multiple_of(t * tile, tile), tile)
-        total = out_ref[:, cols].astype(jnp.float32) + acc_in[n % ACC_SLOTS, :, cols].astype(
-            jnp.float32
-        )
-        out_ref[:, cols] = total.astype(jnp.bfloat16)
-
-    for copy in ring_x(n - 2) + ring_acc(n - 2) + ring_acc(n - 1):
+    for k in range(BANDS):
+        for copy in ring_acc(n - 1, k):
+            copy.wait_recv()
+
+        @pl.loop(0, band // tile)
+        def _(t):
+            cols = pl.ds(pl.multiple_of(k * band + t * tile, tile), tile)
+            total = out_ref[:, cols].astype(jnp.float32) + acc_in[n % ACC_SLOTS, :, cols].astype(
+                jnp.float32
+            )
+            out_ref[:, cols] = total.astype(jnp.bfloat16)
+
+    for copy in ring_x(n - 2):
         copy.wait_send()
+    for k in range(BANDS):
+        for copy in ring_acc(n - 2, k) + ring_acc(n - 1, k):
+            copy.wait_send()
 
 
 def body(
@@ -224,7 +245,6 @@
     meta = jnp.concatenate(
         [high.astype(jnp.bfloat16), low.astype(jnp.bfloat16), act_scale[:, None],
          jnp.zeros((rows, extra - used), jnp.bfloat16)], axis=1)
-    x = jnp.concatenate([act, meta], axis=1)
     bf16 = jnp.bfloat16
     anywhere = pl.BlockSpec(memory_space=pl.ANY)
     vmem = pl.BlockSpec(memory_space=pltpu.VMEM)
@@ -232,7 +252,7 @@
     return pl.pallas_call(
         functools.partial(kernel, n, snake, experts),
         out_shape=jax.ShapeDtypeStruct((rows, width), bf16),
-        in_specs=[anywhere] * 4 + [vmem] * 3,
+        in_specs=[anywhere] * 5 + [vmem] * 3,
         out_specs=vmem,
         scratch_shapes=[
             pltpu.VMEM((X_SLOTS, 2 * rows, width + extra), bf16),
@@ -244,13 +264,13 @@
             pltpu.VMEM((width, hidden), bf16),
             pltpu.VMEM((hidden, width), bf16),
             pltpu.VMEM((2 * rows, hidden), bf16),
-            dma((4,)), dma((2, X_SLOTS)), dma((2, X_SLOTS)),
-            dma((2, 2)), dma((2, ACC_SLOTS)), dma((2, X_SLOTS)), dma((2, 2)),
+            dma((5,)), dma((2, X_SLOTS)), dma((2, X_SLOTS)),
+            dma((2, BANDS, 2)), dma((2, BANDS, ACC_SLOTS)), dma((2, X_SLOTS)), dma((2, 2)),
         ],
         compiler_params=pltpu.CompilerParams(
             collective_id=0, has_side_effects=True, vmem_limit_bytes=62 * 1024 * 1024
         ),
-    )(x, w_gate[0], w_up[0], w_down[0], gate_scale, up_scale, down_row)
+    )(act, meta, w_gate[0], w_up[0], w_down[0], gate_scale, up_scale, down_row)
 
 
 def winds_back(mesh):

time: 299 us -> 295 us (0.987)
  local copies, waits for them, and re-layouts: 8.62 us -> 4.77 us
    concatenate x1, local copies, waits for them, and re-layouts: 3.81 us -> 0.08 us  [body(): jnp.concatenate([high.astype(jnp.bfloat16), low.astype(jnp.bfloat16), act...]
where the time goes in v3:
time: 295 us; the launch traced here: 291 us
  Pallas kernels  284 us (96%)
  local copies, waits for them, and re-layouts  4.77 us (2%)
    pallas_call x1, Pallas kernels, body(): pl.pallas_call(functools.partial(kernel, n, snake, experts), out_shape=ja...  284 us

profile of v3, /device:TPU:13, one launch (start us, length us, event | category | flops | bytes accessed | tf_op | source)
XLA Modules:
  0.0 290.6 jit_solution(7064192753909502944)
XLA Ops:
  0.0 0.0 copy-start
  0.0 0.1 pad.3.clone
  0.1 0.7 select_reduce_fusion
  0.8 0.1 copy-done
  0.9 0.6 constant_dynamic-slice_fusion.down_ref
  1.6 0.1 copy.19
  1.7 0.8 copy.20
  2.5 0.1 copy.17
  2.6 0.1 copy.18
  2.7 0.7 maximum_maximum_fusion.meta_hbm
  3.4 284.4 %shard_map.100 = bf16[128,7168]{1,0:T(8,128)(2,1)} custom-call(bf16[128,7168]{1,0:T(8,128)(2,1)} %x_hbm.1, bf16[128,128]{1,0:T(8,128)(2,1)} %maximum_maximum_fusion.meta_hbm, bf16[7168,512]{1,0:T(8,128)(2,1)} %bitcast.4, bf16[7168,512]{1,0:T(8,128)(2,1)} %bitcast.5, bf16[512,7168]{1,0:T(8,128)(2,1)} %bitcast.6, f32[1,512]{1,0:T(1,128)} %gs_ref.1, ...), custom_call_target="tpu_custom_call" | custom-call | tf_op jit(solution)/shard_map/pallas_call | solution.py:252
  287.8 2.8 copy.22
  (3 shorter events, 0.0 us)
Async XLA Ops:
  0.0 0.9 copy-start

commit v4 on v3

--- a/solution.py
+++ b/solution.py
@@ -11,7 +11,7 @@
 PIECES = 2
 X_SLOTS = 4
 ACC_SLOTS = 3
-BANDS = 2
+BANDS = 4
 
 
 def kernel(
@@ -73,9 +73,11 @@
         return remote(xb.at[a, pl.ds(0, rows)], xb.at[a, pl.ds(rows, rows)],
                       sx_sem.at[0, a], sx_sem.at[1, a], sib)
 
-    def sib_part(s):
+    def sib_part(s, k):
         a = s % 2
-        return remote(sp_out.at[a], sp_in.at[a], sp_sem.at[0, a], sp_sem.at[1, a], sib)
+        cols = pl.ds(k * band, band)
+        return remote(sp_out.at[a, :, cols], sp_in.at[a, :, cols],
+                      sp_sem.at[0, k, a], sp_sem.at[1, k, a], sib)
 
     first = [
         pltpu.make_async_copy(x_hbm, xb.at[0, pl.ds(0, rows), pl.ds(0, width)], load_sem.at[3]),
@@ -102,7 +104,7 @@
         copy.start()
     sib_x(0).start()
 
-    tile = math.gcd(band, 512)
+    tile = band if band % 256 == 0 else math.gcd(band, 256)
     htile = math.gcd(hidden, 256)
 
     def step(s, carry):
@@ -155,31 +157,32 @@
 
             sib_x(s + 1).start()
 
-        @pl.loop(0, width // tile)
-        def _(t):
-            cols = pl.ds(pl.multiple_of(t * tile, tile), tile)
-            part = jnp.dot(hid[...], wd[:, cols], preferred_element_type=jnp.float32)
-            part = (part * down_ref[:, cols] * weight).astype(jnp.bfloat16)
-            acc_out[out_slot, :, cols] = part[:rows]
-            sp_out[out_slot, :, cols] = part[rows:]
-
-        exchange = sib_part(s)
-        exchange.start()
-        exchange.wait()
+        for k in range(BANDS):
+            @pl.loop(0, band // tile)
+            def _(t):
+                cols = pl.ds(pl.multiple_of(k * band + t * tile, tile), tile)
+                part = jnp.dot(hid[...], wd[:, cols], preferred_element_type=jnp.float32)
+                part = (part * down_ref[:, cols] * weight).astype(jnp.bfloat16)
+                acc_out[out_slot, :, cols] = part[:rows]
+                sp_out[out_slot, :, cols] = part[rows:]
+
+            sib_part(s, k).start()
 
         def both(cols):
             return acc_out[out_slot, :, cols].astype(jnp.float32) + sp_in[
                 out_slot, :, cols
             ].astype(jnp.float32)
 
-        @pl.when(s == 0)
-        def _():
-            @pl.loop(0, width // tile)
-            def _(t):
-                cols = pl.ds(pl.multiple_of(t * tile, tile), tile)
-                out_ref[:, cols] = both(cols).astype(jnp.bfloat16)
-
         for k in range(BANDS):
+            sib_part(s, k).wait()
+
+            @pl.when(s == 0)
+            def _():
+                @pl.loop(0, band // tile)
+                def _(t):
+                    cols = pl.ds(pl.multiple_of(k * band + t * tile, tile), tile)
+                    out_ref[:, cols] = both(cols).astype(jnp.bfloat16)
+
             @pl.when(s == 1)
             def _():
                 @pl.loop(0, band // tile)
@@ -265,7 +268,7 @@
             pltpu.VMEM((hidden, width), bf16),
             pltpu.VMEM((2 * rows, hidden), bf16),
             dma((5,)), dma((2, X_SLOTS)), dma((2, X_SLOTS)),
-            dma((2, BANDS, 2)), dma((2, BANDS, ACC_SLOTS)), dma((2, X_SLOTS)), dma((2, 2)),
+            dma((2, BANDS, 2)), dma((2, BANDS, ACC_SLOTS)), dma((2, X_SLOTS)), dma((2, BANDS, 2)),
         ],
         compiler_params=pltpu.CompilerParams(
             collective_id=0, has_side_effects=True, vmem_limit_bytes=62 * 1024 * 1024

time: 295 us -> 295 us (level)
  no operation moved by 1% of the time
where the time goes in v4:
time: 295 us; the launch traced here: 291 us
  Pallas kernels  284 us (96%)
  local copies, waits for them, and re-layouts  4.77 us (2%)
    pallas_call x1, Pallas kernels, body(): pl.pallas_call(functools.partial(kernel, n, snake, experts), out_shape=ja...  284 us

profile of v4, /device:TPU:13, one launch (start us, length us, event | category | flops | bytes accessed | tf_op | source)
XLA Modules:
  0.0 290.6 jit_solution(8251671942914339817)
XLA Ops:
  0.0 0.0 copy-start
  0.0 0.1 pad.3.clone
  0.1 0.7 select_reduce_fusion
  0.8 0.1 copy-done
  0.9 0.6 constant_dynamic-slice_fusion.down_ref
  1.6 0.1 copy.19
  1.7 0.8 copy.20
  2.5 0.1 copy.17
  2.6 0.1 copy.18
  2.7 0.7 maximum_maximum_fusion.meta_hbm
  3.4 284.3 %shard_map.100 = bf16[128,7168]{1,0:T(8,128)(2,1)} custom-call(bf16[128,7168]{1,0:T(8,128)(2,1)} %x_hbm.1, bf16[128,128]{1,0:T(8,128)(2,1)} %maximum_maximum_fusion.meta_hbm, bf16[7168,512]{1,0:T(8,128)(2,1)} %bitcast.4, bf16[7168,512]{1,0:T(8,128)(2,1)} %bitcast.5, bf16[512,7168]{1,0:T(8,128)(2,1)} %bitcast.6, f32[1,512]{1,0:T(1,128)} %gs_ref.1, ...), custom_call_target="tpu_custom_call" | custom-call | tf_op jit(solution)/shard_map/pallas_call | solution.py:255
  287.7 2.8 copy.22
  (3 shorter events, 0.0 us)
Async XLA Ops:
  0.0 0.9 copy-start
